TPU v7x, 256 devices: a whole 4x4x8 slice. The times are simulated.
256 devices in a mesh: patch: 64 (over z, y, core), sample: 4 (over x).
Axes of the slice: x: 4, y: 4, z: 8, core: 2. Of those that a mesh axis runs over, the one named last changes fastest.
Arguments:
- features: bfloat16 [4, 32768, 512], P('sample', 'patch'), may hold values from -600 to 600
- cotangent: bfloat16 [4, 32768, 512], P('sample', 'patch'), may hold values from -6 to 6
- weight_qkv: bfloat16 [512, 1536], replicated, may hold values from -5 to 5
- weight_out: bfloat16 [512, 512], replicated, may hold values from -0.25 to 0.25
- key_tiles: int32 [256, 8], replicated, may hold values from 0 to 255, as said below
- tile_valid: int32 [256, 8], replicated, may hold values from 0 to 1, as said below
Outputs:
- grad_features: bfloat16 [4, 32768, 512], P('sample', 'patch')
- grad_qkv: float32 [512, 1536], replicated
- grad_out: float32 [512, 512], replicated
Inputs may be any that keep to these rules, and one draw needn't show every extreme that they name: `key_tiles`: row g names 8 distinct tile ids. A tile's patch is its id // 4. The first id is g itself, the next 3 are other tiles of g's patch, and the last 4 lie one each in the patches at offsets -2 to 2 other than 0 around the cycle of patches, in rising order of offset. Over the rows of one patch exactly 2 distinct tiles of each such neighbouring patch are named. `tile_valid`: column 0 is always 1.
All inputs are finite; a program needn't handle non-finite values.
Results may differ from a plain program's by a relative error of at most 0.0088.
Values may be sent and summed in bfloat16 or wider, within the bound.
A program may use at most 192 MiB of HBM per device.

v0:
```python
from functools import partial
import math
import jax
import jax.numpy as jnp
from jax import lax
from jax.sharding import PartitionSpec as P

HEADS = 4
TILE = 128
NB = 8
REACH = 2
epsilon = 1e-06


def from_behind(value, axis, steps):
    count = lax.axis_size(axis)
    pairs = [(source, (source + steps) % count) for source in range(count)]
    return lax.ppermute(value, axis, pairs)


def tile_backward(query_tile, pair_tiles, live_flags, grad_tile, head_count):
    row_count = query_tile.shape[0]
    model_width = query_tile.shape[1]
    head_width = model_width // head_count
    scaling = head_width ** (-0.5)
    key_heads = pair_tiles[:, :, :model_width].reshape(-1, head_count, head_width)
    value_heads = pair_tiles[:, :, model_width:].reshape(-1, head_count, head_width)
    query_heads = query_tile.reshape(row_count, head_count, head_width)
    grad_heads = grad_tile.reshape(row_count, head_count, head_width)
    scores = (
        jnp.einsum("qhd,khd->hqk", query_heads, key_heads, preferred_element_type=jnp.float32)
        * scaling
    )
    live_mask = jnp.repeat(live_flags > 0, pair_tiles.shape[1])
    scores = jnp.where(live_mask[None, None, :], scores, -jnp.inf)
    highest = jnp.max(scores, -1, keepdims=True)
    expanded = jnp.exp(scores - highest)
    attention = expanded / jnp.sum(expanded, -1, keepdims=True)
    attention_low = attention.astype(jnp.bfloat16)
    attended = jnp.einsum(
        "hqk,khd->qhd", attention_low, value_heads, preferred_element_type=jnp.float32
    )
    attended = attended.astype(jnp.bfloat16).reshape(row_count, model_width)
    dprob = jnp.einsum("qhd,khd->hqk", grad_heads, value_heads, preferred_element_type=jnp.float32)
    centre = jnp.sum(attention * dprob, -1, keepdims=True)
    dscore = (attention * (dprob - centre) * scaling).astype(jnp.bfloat16)
    dquery = jnp.einsum(
        "hqk,khd->qhd", dscore, key_heads, preferred_element_type=jnp.float32
    ).reshape(row_count, model_width)
    dkey = jnp.einsum("hqk,qhd->khd", dscore, query_heads, preferred_element_type=jnp.float32)
    dvalue = jnp.einsum(
        "hqk,qhd->khd", attention_low, grad_heads, preferred_element_type=jnp.float32
    )
    dkey = dkey.reshape(pair_tiles.shape[0], pair_tiles.shape[1], model_width)
    dvalue = dvalue.reshape(pair_tiles.shape[0], pair_tiles.shape[1], model_width)
    return (attended, dquery, jnp.concatenate([dkey, dvalue], -1))


def on_device(features, cotangent, weight_qkv, weight_out, key_tiles, tile_valid):
    patches = lax.axis_size("patch")
    position = lax.axis_index("patch")
    rows_local = features.shape[1]
    model_width = features.shape[2]
    tile_count = rows_local // TILE
    offsets = [shift_by for shift_by in range(-REACH, REACH + 1) if shift_by != 0]
    inputs = features[0].astype(jnp.float32)
    inverse = lax.rsqrt(jnp.mean(inputs * inputs, -1, keepdims=True) + epsilon)
    normed = inputs * inverse
    normed_low = normed.astype(jnp.bfloat16)
    projected = jnp.dot(normed_low, weight_qkv, preferred_element_type=jnp.float32).astype(
        jnp.bfloat16
    )
    queries = projected[:, :model_width]
    pairs_own = projected[:, model_width:].reshape(tile_count, TILE, 2 * model_width)
    grad_rows = cotangent[0]
    grad_attended = jnp.einsum(
        "pe,de->pd", grad_rows, weight_out, preferred_element_type=jnp.float32
    ).astype(jnp.bfloat16)
    my_lists = lax.dynamic_slice_in_dim(key_tiles, position * tile_count, tile_count, 0)
    my_valid = lax.dynamic_slice_in_dim(tile_valid, position * tile_count, tile_count, 0)
    owner_patch = my_lists // tile_count
    within = my_lists % tile_count
    distance = (owner_patch - position) % patches
    distance = jnp.where(distance > patches // 2, distance - patches, distance)
    order_index = jnp.where(distance < 0, distance + REACH, distance + REACH - 1)
    arrivals = []
    for shift_by in offsets:
        arrivals.append(from_behind(pairs_own, "patch", -shift_by))
    buffer = jnp.concatenate([pairs_own] + arrivals, 0)
    slot_ids = jnp.where(distance == 0, within, tile_count + order_index * tile_count + within)
    group_size = math.gcd(4, tile_count)
    step_count = tile_count // group_size
    tile_pass = jax.vmap(partial(tile_backward, head_count=HEADS))
    buffer_count = buffer.shape[0]

    def advance(running, pieces):
        query_group, slot_group, live_group, grad_group = pieces
        flat_slots = slot_group.reshape(-1)
        gathered = jnp.take(buffer, flat_slots, axis=0).reshape(
            group_size, NB, TILE, 2 * model_width
        )
        attended, dquery, dpairs = tile_pass(query_group, gathered, live_group, grad_group)
        running = running.at[flat_slots].add(dpairs.reshape(group_size * NB, TILE, 2 * model_width))
        return (running, (attended, dquery))

    start_sums = jnp.zeros((buffer_count, TILE, 2 * model_width), jnp.float32)
    scanned = (
        queries.reshape(step_count, group_size, TILE, model_width),
        slot_ids.reshape(step_count, group_size, NB),
        my_valid.reshape(step_count, group_size, NB),
        grad_attended.reshape(step_count, group_size, TILE, model_width),
    )
    totals, (attended_all, dquery_all) = lax.scan(advance, start_sums, scanned)
    grads_own = totals[:tile_count]
    for offset_index, shift_by in enumerate(offsets):
        portion = totals[
            tile_count + offset_index * tile_count : tile_count + (offset_index + 1) * tile_count
        ]
        grads_own = grads_own + from_behind(portion.astype(jnp.bfloat16), "patch", shift_by).astype(
            portion.dtype
        )
    attended_rows = attended_all.reshape(rows_local, model_width)
    grad_projected = jnp.concatenate(
        [
            dquery_all.reshape(rows_local, model_width),
            grads_own.reshape(rows_local, 2 * model_width),
        ],
        1,
    ).astype(jnp.bfloat16)
    grad_normed = jnp.einsum(
        "pe,de->pd", grad_projected, weight_qkv, preferred_element_type=jnp.float32
    )
    grad_inputs = grad_rows.astype(jnp.float32) + inverse * (
        grad_normed - normed * jnp.mean(grad_normed * normed, -1, keepdims=True)
    )
    local_qkv = jnp.einsum(
        "pd,pe->de", normed_low, grad_projected, preferred_element_type=jnp.float32
    )
    local_out = jnp.einsum(
        "pd,pe->de", attended_rows, grad_rows, preferred_element_type=jnp.float32
    )
    summed_qkv, summed_out = lax.psum((local_qkv, local_out), ("patch", "sample"))
    factor = float(lax.axis_size("patch") * lax.axis_size("sample") * rows_local) ** (-0.5)
    return (grad_inputs.astype(jnp.bfloat16)[None], summed_qkv * factor, summed_out * factor)


def solution(mesh):
    placed = (P("sample", "patch", None), P("sample", "patch", None), P(), P(), P(), P())
    return jax.shard_map(
        on_device,
        mesh=mesh,
        in_specs=placed,
        out_specs=(P("sample", "patch", None), P(), P()),
        check_vma=False,
    )
```

profile of v0, /device:TPU:2, one launch (start us, length us, event | category | flops | bytes accessed | tf_op | source)
XLA Modules:
  0.0 587.7 jit_solution(10732911310257279190)
XLA Ops:
  13.6 6.2 %collective-permute-start.2 = (bf16[4,128,1024]{2,1,0:T(8,128)(2,1)}, bf16[4,128,1024]{2,1,0:T(8,128)(2,1)}, u32[]{:S(2)}, u32[]{:S(2)}) collective-permute-start(bf16[4,128,1024]{2,1,0:T(8,128)(2,1)} %bitcast.3), channel_id=1, source_target_pairs={{0,252},{4,0},{8,4},{12,8},{16,12},{20,16},{24,20},{28,24},{32,28}... | collective-permute-start | bytes 3145736 | tf_op jit(solution)/shard_map/ppermute | solution.py:18
  19.8 2.3 collective-permute-start.3
  32.8 11.9 %collective-permute-done = bf16[4,128,1024]{2,1,0:T(8,128)(2,1)} collective-permute-done((bf16[4,128,1024]{2,1,0:T(8,128)(2,1)}, bf16[4,128,1024]{2,1,0:T(8,128)(2,1)}, u32[]{:S(2)}, u32[]{:S(2)}) %collective-permute-start) | collective-permute-done | bytes 1048608 | tf_op jit(solution)/shard_map/ppermute | solution.py:18
  44.7 2.3 constant_dynamic-update-slice_fusion.3
  47.0 8.1 %collective-permute-done.1 = bf16[4,128,1024]{2,1,0:T(8,128)(2,1)} collective-permute-done((bf16[4,128,1024]{2,1,0:T(8,128)(2,1)}, bf16[4,128,1024]{2,1,0:T(8,128)(2,1)}, u32[]{:S(2)}, u32[]{:S(2)}) %collective-permute-start.1) | collective-permute-done | bytes 1048608 | tf_op jit(solution)/shard_map/ppermute | solution.py:18
  61.9 7.6 %gather_fusion = bf16[32,128,1024]{2,1,0:T(8,128)(2,1)} fusion(bf16[20,128,1024]{2,1,0:T(8,128)(2,1)} %constant_dynamic-update-slice_fusion, s32[1024]{0:T(1024)S(1)} %pad_clamp_fusion), kind=kCustom, calls=%fused_computation | custom fusion | bytes 16777344 | tf_op jit(solution)/shard_map/while/body/eval_jaxpr/jit(_take)/gather | solution.py:99
  69.5 7.5 %broadcast_select_fusion = bf16[4,8,128,1024]{3,2,1,0:T(8,128)(2,1)} fusion(bf16[4,8,128,1024]{3,2,1,0:T(8,128)(2,1)} %bitcast.63, pred[4,8]{1,0:T(4,128)(4,1)S(1)} %copy.39), kind=kLoop, calls=%fused_computation.10 | loop fusion | flops 4194304 | bytes 16777248 | tf_op jit(solution)/shard_map/while/body/eval_jaxpr/jit(_take)/select_n | solution.py:99
  77.0 5.9 fusion.70
  82.9 6.9 %reshape.155 = bf16[4,1024,4,128]{3,2,1,0:T(4,128)(2,1)} reshape(bf16[4,8,128,512]{3,2,1,0:T(8,128)(2,1)} %get-tuple-element.44) | data formatting | bytes 8388608 | tf_op jit(solution)/shard_map/while/body/eval_jaxpr/vmap()/reshape | solution.py:26
  89.8 7.6 %copy.57 = bf16[4,1024,4,128]{1,3,2,0:T(8,128)(2,1)} copy(bf16[4,1024,4,128]{3,2,1,0:T(4,128)(2,1)} %reshape.155) | data formatting | bytes 8388608 | tf_op jit(solution)/shard_map/while/body/eval_jaxpr/vmap()/reshape | solution.py:26
  97.3 6.9 %reshape.156 = bf16[4,1024,4,128]{3,2,1,0:T(4,128)(2,1)} reshape(bf16[4,8,128,512]{3,2,1,0:T(8,128)(2,1)} %get-tuple-element.43) | data formatting | bytes 8388608 | tf_op jit(solution)/shard_map/while/body/eval_jaxpr/vmap()/reshape | solution.py:27
  104.2 7.5 %copy.56 = bf16[4,1024,4,128]{1,3,2,0:T(8,128)(2,1)} copy(bf16[4,1024,4,128]{3,2,1,0:T(4,128)(2,1)} %reshape.156) | data formatting | bytes 8388608 | tf_op jit(solution)/shard_map/while/body/eval_jaxpr/vmap()/reshape | solution.py:27
  111.7 6.7 %fusion.73 = f32[4,4,128,1024]{3,2,1,0:T(8,128)} fusion(bf16[4,128,4,128]{1,3,2,0:T(8,128)(2,1)S(1)} %copy.51, bf16[4,1024,4,128]{1,3,2,0:T(8,128)(2,1)} %copy.56), kind=kOutput, calls=%fused_computation.98 | convolution fusion | flops 536870912 | bytes 13107200 | tf_op jit(solution)/shard_map/while/body/eval_jaxpr/vmap(qhd,khd->hqk)/dot_general | solution.py:44
  118.4 8.8 %fusion.72 = (f32[4,4,128]{2,1,0:T(4,128)S(1)}, f32[4,4,128,1024]{3,2,1,0:T(8,128)}) fusion(pred[4,1024]{1,0:T(4,128)(4,1)S(1)} %bitcast.70, bf16[4,128,4,128]{1,3,2,0:T(8,128)(2,1)} %copy.49, bf16[4,1024,4,128]{1,3,2,0:T(8,128)(2,1)} %copy.57), kind=kOutput, calls=%fused_computation.97 | convolution fusion | flops 545260544 | bytes 13119488 | tf_op jit(solution)/shard_map/while/body/eval_jaxpr/vmap()/sub | solution.py:37
  127.2 7.9 %convolution_bitcast_fusion = f32[4,1024,4,128]{1,3,2,0:T(8,128)} fusion(bf16[4,128,4,128]{1,3,2,0:T(8,128)(2,1)S(1)} %copy.51, f32[4,4,128,1024]{3,2,1,0:T(8,128)} %get-tuple-element.50, f32[4,4,128]{2,1,0:T(4,128)S(1)} %get-tuple-element.49), kind=kOutput, calls=%fused_computation.19 | convolution fusion | flops 541065216 | bytes 17309696 | tf_op jit(solution)/shard_map/while/body/eval_jaxpr/vmap(hqk,qhd->khd)/dot_general | solution.py:51
  135.1 24.0 %fusion.15 = f32[4,1024,4,128]{1,3,2,0:T(8,128)} fusion(bf16[4,128,4,128]{1,3,2,0:T(8,128)(2,1)} %copy.49, f32[4,4,128,1024]{3,2,1,0:T(8,128)} %fusion.73, f32[4,4,128,1024]{3,2,1,0:T(8,128)} %get-tuple-element.50, f32[4,4,128]{2,1,0:T(4,128)S(1)} %get-tuple-element.49), kind=kOutput, calls=%fused_computation.18 | convolution fusion | flops 551554048 | bytes 25698304 | tf_op jit(solution)/shard_map/while/body/eval_jaxpr/vmap(hqk,qhd->khd)/dot_general | solution.py:50
  159.1 9.9 %copy.50 = f32[4,1024,4,128]{3,2,1,0:T(4,128)} copy(f32[4,1024,4,128]{1,3,2,0:T(8,128)} %fusion.15) | data formatting | bytes 16777216 | tf_op jit(solution)/shard_map/while/body/eval_jaxpr/vmap(hqk,qhd->khd)/transpose | solution.py:50
  169.0 10.3 %concatenate.17 = f32[32,128,512]{2,1,0:T(8,128)} reshape(f32[4,1024,4,128]{3,2,1,0:T(4,128)} %copy.50) | data formatting | bytes 16777216 | tf_op jit(solution)/shard_map/while/body/eval_jaxpr/vmap()/concatenate | solution.py:56
  179.3 9.9 %copy.52 = f32[4,1024,4,128]{3,2,1,0:T(4,128)} copy(f32[4,1024,4,128]{1,3,2,0:T(8,128)} %convolution_bitcast_fusion) | data formatting | bytes 16777216 | tf_op jit(solution)/shard_map/while/body/eval_jaxpr/vmap(hqk,qhd->khd)/transpose | solution.py:51
  189.1 10.3 %concatenate.18 = f32[32,128,512]{2,1,0:T(8,128)} reshape(f32[4,1024,4,128]{3,2,1,0:T(4,128)} %copy.52) | data formatting | bytes 16777216 | tf_op jit(solution)/shard_map/while/body/eval_jaxpr/vmap()/concatenate | solution.py:56
  199.4 11.7 %pad_maximum_fusion = f32[32,128,1024]{2,1,0:T(8,128)} fusion(f32[32,128,512]{2,1,0:T(8,128)} %concatenate.18, f32[32,128,512]{2,1,0:T(8,128)} %concatenate.17), kind=kLoop, calls=%fused_computation.4 | loop fusion | flops 4194304 | bytes 33554432 | tf_op jit(solution)/shard_map/while/body/eval_jaxpr/vmap()/concatenate | solution.py:56
  211.1 5.2 broadcast_in_dim.64
  216.3 36.2 %scatter_fusion = f32[20,128,1024]{2,1,0:T(8,128)} fusion(f32[20,128,1024]{2,1,0:T(8,128)} %broadcast_in_dim.64, s32[32]{0:T(128)S(1)} %fusion.61, f32[32,128,1024]{2,1,0:T(8,128)} %pad_maximum_fusion), kind=kCustom, calls=%fused_computation.1 | custom fusion | flops 4194304 | bytes 50331776 | tf_op jit(solution)/shard_map/while/body/eval_jaxpr/scatter-add | solution.py:103
  252.5 4.8 convert.17
  257.3 2.3 fusion.71
  262.2 4.7 fusion.34
  268.0 22.9 %fusion.37 = bf16[4,128,4,128]{1,3,2,0:T(8,128)(2,1)S(1)} fusion(bf16[4,1024,4,128]{1,3,2,0:T(8,128)(2,1)} %copy.57, f32[4,4,128,1024]{3,2,1,0:T(8,128)} %fusion.73, f32[4,4,128,1024]{3,2,1,0:T(8,128)} %get-tuple-element.50, f32[4,4,128]{2,1,0:T(4,128)S(1)} %get-tuple-element.49), kind=kOutput, calls=%fused_computation.40 | convolution fusion | flops 551816192 | bytes 21504000 | tf_op jit(solution)/shard_map/while/body/eval_jaxpr/vmap(hqk,khd->qhd)/dot_general | solution.py:47
  293.1 2.5 fusion.49
  295.6 3.8 fusion.21
  300.4 2.6 fusion.46
  307.7 268.1 %all-reduce.3.cloned.1.call-done = (f32[512,1536]{1,0:T(8,128)}, f32[512,512]{1,0:T(8,128)}) async-done(((f32[512,1536]{1,0:T(8,128)}, f32[512,512]{1,0:T(8,128)}), (f32[512,1536]{1,0:T(8,128)}, f32[512,512]{1,0:T(8,128)})) %all-reduce.3.cloned.1.call-update) | async-done | bytes 4194320 | tf_op jit(solution)/shard_map/psum | solution.py:142
  575.8 4.0 broadcast_multiply_fusion
  (65 shorter events, 36.3 us)
Async XLA Ops:
  7.2 1.6 copy-start
  7.2 15.0 %copy-start.7 = (s32[256,8]{0,1:T(8,128)S(1)}, s32[256,8]{0,1:T(8,128)}, u32[]{:S(2)}) copy-start(s32[256,8]{0,1:T(8,128)} %param.10) | copy-start | bytes 24580
  7.2 15.0 %copy-start.8 = (s32[256,8]{0,1:T(8,128)S(1)}, s32[256,8]{0,1:T(8,128)}, u32[]{:S(2)}) copy-start(s32[256,8]{0,1:T(8,128)} %param.11) | copy-start | bytes 24580
  7.2 568.6 %all-reduce.3.cloned.1.call-start = ((), (), s32[]{:S(2)}) async-start(), calls=%async_computation | async-start | bytes 8388608 | tf_op jit(solution)/shard_map/psum | solution.py:142
  8.8 18.0 %copy-start.2 = (bf16[1,512,512]{2,1,0:T(8,128)(2,1)S(1)}, bf16[1,512,512]{2,1,0:T(8,128)(2,1)}, u32[]{:S(2)}) copy-start(bf16[1,512,512]{2,1,0:T(8,128)(2,1)} %param.7) | copy-start | bytes 1572868
  9.8 1.1 copy-start.5
  12.1 32.6 %collective-permute-start = (bf16[4,128,1024]{2,1,0:T(8,128)(2,1)}, bf16[4,128,1024]{2,1,0:T(8,128)(2,1)}, u32[]{:S(2)}, u32[]{:S(2)}) collective-permute-start(bf16[4,128,1024]{2,1,0:T(8,128)(2,1)} %bitcast.3), channel_id=1, source_target_pairs={{0,8},{4,12},{8,16},{12,20},{16,24},{20,28},{24,32},{28,36},{32,40... | collective-permute-start | bytes 3145736 | tf_op jit(solution)/shard_map/ppermute | solution.py:18
  13.6 41.4 %collective-permute-start.1 = (bf16[4,128,1024]{2,1,0:T(8,128)(2,1)}, bf16[4,128,1024]{2,1,0:T(8,128)(2,1)}, u32[]{:S(2)}, u32[]{:S(2)}) collective-permute-start(bf16[4,128,1024]{2,1,0:T(8,128)(2,1)} %bitcast.3), channel_id=1, source_target_pairs={{0,4},{4,8},{8,12},{12,16},{16,20},{20,24},{24,28},{28,32},{32,36}... | collective-permute-start | bytes 3145736 | tf_op jit(solution)/shard_map/ppermute | solution.py:18
  13.6 43.7 %collective-permute-start.2 = (bf16[4,128,1024]{2,1,0:T(8,128)(2,1)}, bf16[4,128,1024]{2,1,0:T(8,128)(2,1)}, u32[]{:S(2)}, u32[]{:S(2)}) collective-permute-start(bf16[4,128,1024]{2,1,0:T(8,128)(2,1)} %bitcast.3), channel_id=1, source_target_pairs={{0,252},{4,0},{8,4},{12,8},{16,12},{20,16},{24,20},{28,24},{32,28}... | collective-permute-start | bytes 3145736 | tf_op jit(solution)/shard_map/ppermute | solution.py:18
  19.8 39.8 %collective-permute-start.3 = (bf16[4,128,1024]{2,1,0:T(8,128)(2,1)}, bf16[4,128,1024]{2,1,0:T(8,128)(2,1)}, u32[]{:S(2)}, u32[]{:S(2)}) collective-permute-start(bf16[4,128,1024]{2,1,0:T(8,128)(2,1)} %bitcast.3), channel_id=1, source_target_pairs={{0,248},{4,252},{8,0},{12,4},{16,8},{20,12},{24,16},{28,20},{32,24... | collective-permute-start | bytes 3145736 | tf_op jit(solution)/shard_map/ppermute | solution.py:18
  257.3 4.9 copy-start.1
  259.7 35.9 %collective-permute-start.4 = (bf16[4,128,1024]{2,1,0:T(8,128)(2,1)}, bf16[4,128,1024]{2,1,0:T(8,128)(2,1)}, u32[]{:S(2)}, u32[]{:S(2)}) collective-permute-start(bf16[4,128,1024]{2,1,0:T(8,128)(2,1)} %get-tuple-element.45), channel_id=1, source_target_pairs={{0,248},{4,252},{8,0},{12,4},{16,8},{20,12},{24,16},{28,20},{32,24... | collective-permute-start | bytes 3145736 | tf_op jit(solution)/shard_map/ppermute | solution.py:18
  261.5 34.1 %collective-permute-start.5 = (bf16[4,128,1024]{2,1,0:T(8,128)(2,1)}, bf16[4,128,1024]{2,1,0:T(8,128)(2,1)}, u32[]{:S(2)}, u32[]{:S(2)}) collective-permute-start(bf16[4,128,1024]{2,1,0:T(8,128)(2,1)} %get-tuple-element.48), channel_id=1, source_target_pairs={{0,252},{4,0},{8,4},{12,8},{16,12},{20,16},{24,20},{28,24},{32,28}... | collective-permute-start | bytes 3145736 | tf_op jit(solution)/shard_map/ppermute | solution.py:18
  261.5 34.1 %collective-permute-start.6 = (bf16[4,128,1024]{2,1,0:T(8,128)(2,1)}, bf16[4,128,1024]{2,1,0:T(8,128)(2,1)}, u32[]{:S(2)}, u32[]{:S(2)}) collective-permute-start(bf16[4,128,1024]{2,1,0:T(8,128)(2,1)} %get-tuple-element.47), channel_id=1, source_target_pairs={{0,4},{4,8},{8,12},{12,16},{16,20},{20,24},{24,28},{28,32},{32,36}... | collective-permute-start | bytes 3145736 | tf_op jit(solution)/shard_map/ppermute | solution.py:18
  262.0 33.6 %collective-permute-start.7 = (bf16[4,128,1024]{2,1,0:T(8,128)(2,1)}, bf16[4,128,1024]{2,1,0:T(8,128)(2,1)}, u32[]{:S(2)}, u32[]{:S(2)}) collective-permute-start(bf16[4,128,1024]{2,1,0:T(8,128)(2,1)} %get-tuple-element.46), channel_id=1, source_target_pairs={{0,8},{4,12},{8,16},{12,20},{16,24},{20,28},{24,32},{28,36},{32,40... | collective-permute-start | bytes 3145736 | tf_op jit(solution)/shard_map/ppermute | solution.py:18
  299.4 1.0 copy-start.3
  304.0 2.3 copy-start.4
  575.8 4.0 copy-start.6
Sparse Core Ops, SparseCore 0:
  303.2 272.6 all-reduce.2
where the time goes:
time: 590 us; the launch traced here: 588 us
  waiting for transfers between devices  288 us (49%)
  local copies, waits for them, and re-layouts  118 us (20%)
  matrix products  84.9 us (14%)
  other arithmetic  69.6 us (12%)
  between operations  14.2 us (2%)
  starting transfers between devices  12.7 us (2%)
    psum x1, waiting for transfers between devices, on_device(): lax.psum((local_qkv, local_out), ('patch', 'sample'))  268 us
    scatter-add x1, other arithmetic, advance(): running.at[flat_slots]  36.2 us
    dot_general x1, matrix products, tile_backward(): jnp.einsum('hqk,qhd->khd', dscore, query_heads, preferred_element_type=jn...  24 us
    dot_general x1, matrix products, tile_backward(): jnp.einsum('hqk,khd->qhd', dscore, key_heads, preferred_element_type=jnp....  22.9 us
    concatenate x2, local copies, waits for them, and re-layouts, tile_backward(): return (attended, dquery, jnp.concatenate([dkey, dvalue], -1))  20.6 us
    ppermute x8, waiting for transfers between devices, from_behind(): return lax.ppermute(value, axis, pairs)  20 us
    unnamed x28, local copies, waits for them, and re-layouts  15.8 us
    reshape x2, local copies, waits for them, and re-layouts, tile_backward(): pair_tiles[:, :, :model_width].reshape(-1, head_count, head_width)  14.5 us
  transfers between devices with their start and end apart: 9, of which 3 were waited for; matrix products, arithmetic and copies ran while one was open for 9% of the time, Pallas kernels for 0%

commit v1 on v0

--- a/solution.py
+++ b/solution.py
@@ -139,7 +139,7 @@
     local_out = jnp.einsum(
         "pd,pe->de", attended_rows, grad_rows, preferred_element_type=jnp.float32
     )
-    summed_qkv, summed_out = lax.psum((local_qkv, local_out), ("patch", "sample"))
+    summed_qkv, summed_out = lax.psum(lax.psum((local_qkv, local_out), "sample"), "patch")
     factor = float(lax.axis_size("patch") * lax.axis_size("sample") * rows_local) ** (-0.5)
     return (grad_inputs.astype(jnp.bfloat16)[None], summed_qkv * factor, summed_out * factor)
 

time: 590 us -> 619 us (1.049)
  waiting for transfers between devices: 288 us -> 317 us
    psum x1 -> x2, waiting for transfers between devices: 268 us -> 297 us  [the longest x1 196 us: on_device(): lax.psum(lax.psum((local_qkv, local_out), 'sample'), 'patch')]
  transfers between devices with their start and end apart: 9 -> 10, of which waited for: 3 -> 4; matrix products, arithmetic and copies ran while one was open for 9% -> 9% of each run, Pallas kernels for 0% -> 0%
where the time goes in v1:
time: 619 us; the launch traced here: 617 us
  waiting for transfers between devices  317 us (51%)
  local copies, waits for them, and re-layouts  118 us (19%)
  matrix products  84.9 us (14%)
  other arithmetic  69.5 us (11%)
  between operations  14.2 us (2%)
  starting transfers between devices  12.7 us (2%)
    psum x1, waiting for transfers between devices, on_device(): lax.psum(lax.psum((local_qkv, local_out), 'sample'), 'patch')  196 us
    psum x1, waiting for transfers between devices, on_device(): lax.psum((local_qkv, local_out), 'sample')  101 us
    scatter-add x1, other arithmetic, advance(): running.at[flat_slots]  36.1 us
    dot_general x1, matrix products, tile_backward(): jnp.einsum('hqk,qhd->khd', dscore, query_heads, preferred_element_type=jn...  24 us
    dot_general x1, matrix products, tile_backward(): jnp.einsum('hqk,khd->qhd', dscore, key_heads, preferred_element_type=jnp....  22.9 us
    concatenate x2, local copies, waits for them, and re-layouts, tile_backward(): return (attended, dquery, jnp.concatenate([dkey, dvalue], -1))  20.6 us
    ppermute x8, waiting for transfers between devices, from_behind(): return lax.ppermute(value, axis, pairs)  20 us
    unnamed x28, local copies, waits for them, and re-layouts  15.8 us
  transfers between devices with their start and end apart: 10, of which 4 were waited for; matrix products, arithmetic and copies ran while one was open for 9% of the time, Pallas kernels for 0%

profile of v1, /device:TPU:2, one launch (start us, length us, event | category | flops | bytes accessed | tf_op | source)
XLA Modules:
  0.0 616.8 jit_solution(17182172711225214792)
XLA Ops:
  13.6 6.2 %collective-permute-start.2 = (bf16[4,128,1024]{2,1,0:T(8,128)(2,1)}, bf16[4,128,1024]{2,1,0:T(8,128)(2,1)}, u32[]{:S(2)}, u32[]{:S(2)}) collective-permute-start(bf16[4,128,1024]{2,1,0:T(8,128)(2,1)} %bitcast.3), channel_id=1, source_target_pairs={{0,252},{4,0},{8,4},{12,8},{16,12},{20,16},{24,20},{28,24},{32,28}... | collective-permute-start | bytes 3145736 | tf_op jit(solution)/shard_map/ppermute | solution.py:18
  19.8 2.3 collective-permute-start.3
  32.8 11.9 %collective-permute-done = bf16[4,128,1024]{2,1,0:T(8,128)(2,1)} collective-permute-done((bf16[4,128,1024]{2,1,0:T(8,128)(2,1)}, bf16[4,128,1024]{2,1,0:T(8,128)(2,1)}, u32[]{:S(2)}, u32[]{:S(2)}) %collective-permute-start) | collective-permute-done | bytes 1048608 | tf_op jit(solution)/shard_map/ppermute | solution.py:18
  47.0 8.1 %collective-permute-done.1 = bf16[4,128,1024]{2,1,0:T(8,128)(2,1)} collective-permute-done((bf16[4,128,1024]{2,1,0:T(8,128)(2,1)}, bf16[4,128,1024]{2,1,0:T(8,128)(2,1)}, u32[]{:S(2)}, u32[]{:S(2)}) %collective-permute-start.1) | collective-permute-done | bytes 1048608 | tf_op jit(solution)/shard_map/ppermute | solution.py:18
  61.9 7.6 %gather_fusion = bf16[32,128,1024]{2,1,0:T(8,128)(2,1)} fusion(bf16[20,128,1024]{2,1,0:T(8,128)(2,1)} %constant_dynamic-update-slice_fusion, s32[1024]{0:T(1024)S(1)} %pad_clamp_fusion), kind=kCustom, calls=%fused_computation | custom fusion | bytes 16777344 | tf_op jit(solution)/shard_map/while/body/eval_jaxpr/jit(_take)/gather | solution.py:99
  69.5 7.5 %broadcast_select_fusion = bf16[4,8,128,1024]{3,2,1,0:T(8,128)(2,1)} fusion(bf16[4,8,128,1024]{3,2,1,0:T(8,128)(2,1)} %bitcast.63, pred[4,8]{1,0:T(4,128)(4,1)S(1)} %copy.39), kind=kLoop, calls=%fused_computation.10 | loop fusion | flops 4194304 | bytes 16777248 | tf_op jit(solution)/shard_map/while/body/eval_jaxpr/jit(_take)/select_n | solution.py:99
  77.0 5.9 fusion.70
  82.8 6.9 %reshape.155 = bf16[4,1024,4,128]{3,2,1,0:T(4,128)(2,1)} reshape(bf16[4,8,128,512]{3,2,1,0:T(8,128)(2,1)} %get-tuple-element.46) | data formatting | bytes 8388608 | tf_op jit(solution)/shard_map/while/body/eval_jaxpr/vmap()/reshape | solution.py:26
  89.8 7.5 %copy.57 = bf16[4,1024,4,128]{1,3,2,0:T(8,128)(2,1)} copy(bf16[4,1024,4,128]{3,2,1,0:T(4,128)(2,1)} %reshape.155) | data formatting | bytes 8388608 | tf_op jit(solution)/shard_map/while/body/eval_jaxpr/vmap()/reshape | solution.py:26
  97.3 6.9 %reshape.156 = bf16[4,1024,4,128]{3,2,1,0:T(4,128)(2,1)} reshape(bf16[4,8,128,512]{3,2,1,0:T(8,128)(2,1)} %get-tuple-element.45) | data formatting | bytes 8388608 | tf_op jit(solution)/shard_map/while/body/eval_jaxpr/vmap()/reshape | solution.py:27
  104.2 7.5 %copy.56 = bf16[4,1024,4,128]{1,3,2,0:T(8,128)(2,1)} copy(bf16[4,1024,4,128]{3,2,1,0:T(4,128)(2,1)} %reshape.156) | data formatting | bytes 8388608 | tf_op jit(solution)/shard_map/while/body/eval_jaxpr/vmap()/reshape | solution.py:27
  111.7 6.7 %fusion.73 = f32[4,4,128,1024]{3,2,1,0:T(8,128)} fusion(bf16[4,128,4,128]{1,3,2,0:T(8,128)(2,1)S(1)} %copy.51, bf16[4,1024,4,128]{1,3,2,0:T(8,128)(2,1)} %copy.56), kind=kOutput, calls=%fused_computation.98 | convolution fusion | flops 536870912 | bytes 13107200 | tf_op jit(solution)/shard_map/while/body/eval_jaxpr/vmap(qhd,khd->hqk)/dot_general | solution.py:44
  118.4 8.8 %fusion.72 = (f32[4,4,128]{2,1,0:T(4,128)S(1)}, f32[4,4,128,1024]{3,2,1,0:T(8,128)}) fusion(pred[4,1024]{1,0:T(4,128)(4,1)S(1)} %bitcast.70, bf16[4,128,4,128]{1,3,2,0:T(8,128)(2,1)} %copy.49, bf16[4,1024,4,128]{1,3,2,0:T(8,128)(2,1)} %copy.57), kind=kOutput, calls=%fused_computation.97 | convolution fusion | flops 545260544 | bytes 13119488 | tf_op jit(solution)/shard_map/while/body/eval_jaxpr/vmap()/sub | solution.py:37
  127.2 8.0 %convolution_bitcast_fusion = f32[4,1024,4,128]{1,3,2,0:T(8,128)} fusion(bf16[4,128,4,128]{1,3,2,0:T(8,128)(2,1)S(1)} %copy.51, f32[4,4,128,1024]{3,2,1,0:T(8,128)} %get-tuple-element.52, f32[4,4,128]{2,1,0:T(4,128)S(1)} %get-tuple-element.51), kind=kOutput, calls=%fused_computation.19 | convolution fusion | flops 541065216 | bytes 17309696 | tf_op jit(solution)/shard_map/while/body/eval_jaxpr/vmap(hqk,qhd->khd)/dot_general | solution.py:51
  135.1 24.0 %fusion.15 = f32[4,1024,4,128]{1,3,2,0:T(8,128)} fusion(bf16[4,128,4,128]{1,3,2,0:T(8,128)(2,1)} %copy.49, f32[4,4,128,1024]{3,2,1,0:T(8,128)} %fusion.73, f32[4,4,128,1024]{3,2,1,0:T(8,128)} %get-tuple-element.52, f32[4,4,128]{2,1,0:T(4,128)S(1)} %get-tuple-element.51), kind=kOutput, calls=%fused_computation.18 | convolution fusion | flops 551554048 | bytes 25698304 | tf_op jit(solution)/shard_map/while/body/eval_jaxpr/vmap(hqk,qhd->khd)/dot_general | solution.py:50
  159.1 9.9 %copy.50 = f32[4,1024,4,128]{3,2,1,0:T(4,128)} copy(f32[4,1024,4,128]{1,3,2,0:T(8,128)} %fusion.15) | data formatting | bytes 16777216 | tf_op jit(solution)/shard_map/while/body/eval_jaxpr/vmap(hqk,qhd->khd)/transpose | solution.py:50
  169.0 10.3 %concatenate.17 = f32[32,128,512]{2,1,0:T(8,128)} reshape(f32[4,1024,4,128]{3,2,1,0:T(4,128)} %copy.50) | data formatting | bytes 16777216 | tf_op jit(solution)/shard_map/while/body/eval_jaxpr/vmap()/concatenate | solution.py:56
  179.3 9.9 %copy.52 = f32[4,1024,4,128]{3,2,1,0:T(4,128)} copy(f32[4,1024,4,128]{1,3,2,0:T(8,128)} %convolution_bitcast_fusion) | data formatting | bytes 16777216 | tf_op jit(solution)/shard_map/while/body/eval_jaxpr/vmap(hqk,qhd->khd)/transpose | solution.py:51
  189.1 10.3 %concatenate.18 = f32[32,128,512]{2,1,0:T(8,128)} reshape(f32[4,1024,4,128]{3,2,1,0:T(4,128)} %copy.52) | data formatting | bytes 16777216 | tf_op jit(solution)/shard_map/while/body/eval_jaxpr/vmap()/concatenate | solution.py:56
  199.4 11.7 %pad_maximum_fusion = f32[32,128,1024]{2,1,0:T(8,128)} fusion(f32[32,128,512]{2,1,0:T(8,128)} %concatenate.18, f32[32,128,512]{2,1,0:T(8,128)} %concatenate.17), kind=kLoop, calls=%fused_computation.4 | loop fusion | flops 4194304 | bytes 33554432 | tf_op jit(solution)/shard_map/while/body/eval_jaxpr/vmap()/concatenate | solution.py:56
  211.1 5.2 broadcast_in_dim.64
  216.3 36.1 %scatter_fusion = f32[20,128,1024]{2,1,0:T(8,128)} fusion(f32[20,128,1024]{2,1,0:T(8,128)} %broadcast_in_dim.64, s32[32]{0:T(128)S(1)} %fusion.61, f32[32,128,1024]{2,1,0:T(8,128)} %pad_maximum_fusion), kind=kCustom, calls=%fused_computation.1 | custom fusion | flops 4194304 | bytes 50331776 | tf_op jit(solution)/shard_map/while/body/eval_jaxpr/scatter-add | solution.py:103
  252.5 4.8 convert.17
  257.3 2.3 fusion.71
  262.2 4.7 fusion.34
  268.0 22.9 %fusion.37 = bf16[4,128,4,128]{1,3,2,0:T(8,128)(2,1)S(1)} fusion(bf16[4,1024,4,128]{1,3,2,0:T(8,128)(2,1)} %copy.57, f32[4,4,128,1024]{3,2,1,0:T(8,128)} %fusion.73, f32[4,4,128,1024]{3,2,1,0:T(8,128)} %get-tuple-element.52, f32[4,4,128]{2,1,0:T(4,128)S(1)} %get-tuple-element.51), kind=kOutput, calls=%fused_computation.40 | convolution fusion | flops 551816192 | bytes 21504000 | tf_op jit(solution)/shard_map/while/body/eval_jaxpr/vmap(hqk,khd->qhd)/dot_general | solution.py:47
  293.1 2.5 fusion.49
  295.6 3.8 fusion.21
  300.4 2.7 fusion.46
  303.1 100.7 %all-reduce.7.cloned.1.call-done = (f32[512,1536]{1,0:T(8,128)}, f32[512,512]{1,0:T(8,128)}) async-done(((f32[512,1536]{1,0:T(8,128)}, f32[512,512]{1,0:T(8,128)}), (f32[512,1536]{1,0:T(8,128)}, f32[512,512]{1,0:T(8,128)})) %all-reduce.7.cloned.1.call-update) | async-done | bytes 4194320 | tf_op jit(solution)/shard_map/psum | solution.py:142
  408.5 196.5 %all-reduce.5.cloned.1.call-done = (f32[512,1536]{1,0:T(8,128)}, f32[512,512]{1,0:T(8,128)}) async-done(((f32[512,1536]{1,0:T(8,128)}, f32[512,512]{1,0:T(8,128)}), (f32[512,1536]{1,0:T(8,128)}, f32[512,512]{1,0:T(8,128)})) %all-reduce.5.cloned.1.call-update) | async-done | bytes 4194320 | tf_op jit(solution)/shard_map/psum | solution.py:142
  605.0 4.0 broadcast_multiply_fusion
  (68 shorter events, 38.7 us)
Async XLA Ops:
  7.2 1.6 copy-start
  7.2 15.0 %copy-start.7 = (s32[256,8]{0,1:T(8,128)S(1)}, s32[256,8]{0,1:T(8,128)}, u32[]{:S(2)}) copy-start(s32[256,8]{0,1:T(8,128)} %param.10) | copy-start | bytes 24580
  7.2 15.0 %copy-start.8 = (s32[256,8]{0,1:T(8,128)S(1)}, s32[256,8]{0,1:T(8,128)}, u32[]{:S(2)}) copy-start(s32[256,8]{0,1:T(8,128)} %param.11) | copy-start | bytes 24580
  7.2 396.6 %all-reduce.7.cloned.1.call-start = ((), (), s32[]{:S(2)}) async-start(), calls=%async_computation.1 | async-start | bytes 8388608 | tf_op jit(solution)/shard_map/psum | solution.py:142
  8.8 18.0 %copy-start.2 = (bf16[1,512,512]{2,1,0:T(8,128)(2,1)S(1)}, bf16[1,512,512]{2,1,0:T(8,128)(2,1)}, u32[]{:S(2)}) copy-start(bf16[1,512,512]{2,1,0:T(8,128)(2,1)} %param.7) | copy-start | bytes 1572868
  9.8 1.1 copy-start.5
  12.1 32.6 %collective-permute-start = (bf16[4,128,1024]{2,1,0:T(8,128)(2,1)}, bf16[4,128,1024]{2,1,0:T(8,128)(2,1)}, u32[]{:S(2)}, u32[]{:S(2)}) collective-permute-start(bf16[4,128,1024]{2,1,0:T(8,128)(2,1)} %bitcast.3), channel_id=1, source_target_pairs={{0,8},{4,12},{8,16},{12,20},{16,24},{20,28},{24,32},{28,36},{32,40... | collective-permute-start | bytes 3145736 | tf_op jit(solution)/shard_map/ppermute | solution.py:18
  13.6 41.4 %collective-permute-start.1 = (bf16[4,128,1024]{2,1,0:T(8,128)(2,1)}, bf16[4,128,1024]{2,1,0:T(8,128)(2,1)}, u32[]{:S(2)}, u32[]{:S(2)}) collective-permute-start(bf16[4,128,1024]{2,1,0:T(8,128)(2,1)} %bitcast.3), channel_id=1, source_target_pairs={{0,4},{4,8},{8,12},{12,16},{16,20},{20,24},{24,28},{28,32},{32,36}... | collective-permute-start | bytes 3145736 | tf_op jit(solution)/shard_map/ppermute | solution.py:18
  13.6 43.7 %collective-permute-start.2 = (bf16[4,128,1024]{2,1,0:T(8,128)(2,1)}, bf16[4,128,1024]{2,1,0:T(8,128)(2,1)}, u32[]{:S(2)}, u32[]{:S(2)}) collective-permute-start(bf16[4,128,1024]{2,1,0:T(8,128)(2,1)} %bitcast.3), channel_id=1, source_target_pairs={{0,252},{4,0},{8,4},{12,8},{16,12},{20,16},{24,20},{28,24},{32,28}... | collective-permute-start | bytes 3145736 | tf_op jit(solution)/shard_map/ppermute | solution.py:18
  19.8 39.8 %collective-permute-start.3 = (bf16[4,128,1024]{2,1,0:T(8,128)(2,1)}, bf16[4,128,1024]{2,1,0:T(8,128)(2,1)}, u32[]{:S(2)}, u32[]{:S(2)}) collective-permute-start(bf16[4,128,1024]{2,1,0:T(8,128)(2,1)} %bitcast.3), channel_id=1, source_target_pairs={{0,248},{4,252},{8,0},{12,4},{16,8},{20,12},{24,16},{28,20},{32,24... | collective-permute-start | bytes 3145736 | tf_op jit(solution)/shard_map/ppermute | solution.py:18
  257.3 4.9 copy-start.1
  259.6 35.9 %collective-permute-start.4 = (bf16[4,128,1024]{2,1,0:T(8,128)(2,1)}, bf16[4,128,1024]{2,1,0:T(8,128)(2,1)}, u32[]{:S(2)}, u32[]{:S(2)}) collective-permute-start(bf16[4,128,1024]{2,1,0:T(8,128)(2,1)} %get-tuple-element.47), channel_id=1, source_target_pairs={{0,248},{4,252},{8,0},{12,4},{16,8},{20,12},{24,16},{28,20},{32,24... | collective-permute-start | bytes 3145736 | tf_op jit(solution)/shard_map/ppermute | solution.py:18
  261.5 34.0 %collective-permute-start.5 = (bf16[4,128,1024]{2,1,0:T(8,128)(2,1)}, bf16[4,128,1024]{2,1,0:T(8,128)(2,1)}, u32[]{:S(2)}, u32[]{:S(2)}) collective-permute-start(bf16[4,128,1024]{2,1,0:T(8,128)(2,1)} %get-tuple-element.50), channel_id=1, source_target_pairs={{0,252},{4,0},{8,4},{12,8},{16,12},{20,16},{24,20},{28,24},{32,28}... | collective-permute-start | bytes 3145736 | tf_op jit(solution)/shard_map/ppermute | solution.py:18
  261.5 34.0 %collective-permute-start.6 = (bf16[4,128,1024]{2,1,0:T(8,128)(2,1)}, bf16[4,128,1024]{2,1,0:T(8,128)(2,1)}, u32[]{:S(2)}, u32[]{:S(2)}) collective-permute-start(bf16[4,128,1024]{2,1,0:T(8,128)(2,1)} %get-tuple-element.49), channel_id=1, source_target_pairs={{0,4},{4,8},{8,12},{12,16},{16,20},{20,24},{24,28},{28,32},{32,36}... | collective-permute-start | bytes 3145736 | tf_op jit(solution)/shard_map/ppermute | solution.py:18
  262.0 33.5 %collective-permute-start.7 = (bf16[4,128,1024]{2,1,0:T(8,128)(2,1)}, bf16[4,128,1024]{2,1,0:T(8,128)(2,1)}, u32[]{:S(2)}, u32[]{:S(2)}) collective-permute-start(bf16[4,128,1024]{2,1,0:T(8,128)(2,1)} %get-tuple-element.48), channel_id=1, source_target_pairs={{0,8},{4,12},{8,16},{12,20},{16,24},{20,28},{24,32},{28,36},{32,40... | collective-permute-start | bytes 3145736 | tf_op jit(solution)/shard_map/ppermute | solution.py:18
  299.4 1.0 copy-start.3
  303.0 301.9 %all-reduce.5.cloned.1.call-start = ((), (), s32[]{:S(2)}) async-start(), calls=%async_computation | async-start | bytes 8388608 | tf_op jit(solution)/shard_map/psum | solution.py:142
  404.9 2.3 copy-start.4
  605.0 4.0 copy-start.6
Sparse Core Ops, SparseCore 0:
  303.2 100.6 all-reduce.6
  407.9 197.0 all-reduce.4
